TPU v7x, 512 devices: a whole 4x4x16 slice. The times are simulated.
512 devices in a mesh: head: 32 (over z_lo, y, core), seq: 16 (over z_hi, x).
Axes of the slice: x: 4, y: 4, z: 16 (z_hi: 4, z_lo: 4; z = z_hi * 4 + z_lo), core: 2. Of those that a mesh axis runs over, the one named last changes fastest.
Arguments:
- query_rows: bfloat16 [2048, 16384], P('seq', 'head'), may hold values from -512 to 512
- key_rows: bfloat16 [2048, 1024], P('seq'), may hold values from -32 to 32
- value_rows: bfloat16 [2048, 1024], P('seq'), may hold values from -6 to 6
- positions: int32 [2048], P('seq'), may hold values from 0 to 511, as said below
Outputs:
- attended: bfloat16 [2048, 16384], P('seq', 'head')
- hessian: float32 [16384, 16384], P('head', 'seq')
Inputs may be any that keep to these rules, and one draw needn't show every extreme that they name: Each aligned block of 4 spans of 128 tokens is one sequence; each span holds 128 consecutive ascending positions starting at a multiple of 128, and the sequence's spans together hold every position 0 to 511 once.
All inputs are finite; a program needn't handle non-finite values.
Results may differ from a plain program's by a relative error of at most 0.0037.
Values may be sent and summed in bfloat16 or wider, within the bound.
No kernel may reach another device: no remote copies, remote signals or barrier semaphores. Data moves between devices by JAX's collectives and lax.ppermute only.
A program may use at most 64 MiB of HBM per device.

v0:
```python
import jax
import jax.numpy as jnp
from jax import lax
from jax.sharding import PartitionSpec as P

HEADS = 128
KVH = 8
HD = 128
SPANS = 4


def from_partner(value, axis, stride):
    mask = 2**stride
    pairs = [(source, source ^ mask) for source in range(lax.axis_size(axis))]
    return lax.ppermute(value, axis, pairs)


def attend_block(queries, key_block, value_block, visible, local_heads, local_tokens, score_scale):
    scores = jnp.dot(queries, key_block.T, preferred_element_type=jnp.float32) * score_scale
    scores = scores.reshape(local_heads, local_tokens, key_block.shape[0])
    masked = jnp.where(visible[None], scores, -jnp.inf)
    row_top = jnp.max(masked, axis=2, keepdims=True)
    weights = jnp.exp(masked - row_top)
    weight_sum = jnp.sum(weights, axis=2, keepdims=True)
    mixed = jnp.dot(
        weights.astype(jnp.bfloat16).reshape(local_heads * local_tokens, key_block.shape[0]),
        value_block,
        preferred_element_type=jnp.float32,
    )
    return mixed.reshape(local_heads, local_tokens, HD) / weight_sum


def on_device(query_rows, key_rows, value_rows, positions):
    local_tokens = query_rows.shape[0]
    local_heads = query_rows.shape[1] // HD
    group_size = HEADS // KVH
    score_scale = HD ** (-0.5)
    head_index = lax.axis_index("head")
    seq_devices = lax.axis_size("seq")
    head_devices = lax.axis_size("head")
    key_head = head_index * local_heads // group_size
    key_slice = lax.dynamic_slice_in_dim(key_rows, key_head * HD, HD, 1)
    value_slice = lax.dynamic_slice_in_dim(value_rows, key_head * HD, HD, 1)
    queries = jnp.transpose(query_rows.reshape(local_tokens, local_heads, HD), (1, 0, 2))
    queries = queries.reshape(local_heads * local_tokens, HD)
    key_block, value_block, place_block = (key_slice, value_slice, positions)
    for bit in range(SPANS.bit_length() - 1):
        other_keys, other_values, other_places = from_partner(
            (key_block, value_block, place_block), "seq", bit
        )
        key_block = jnp.concatenate([key_block, other_keys], axis=0)
        value_block = jnp.concatenate([value_block, other_values], axis=0)
        place_block = jnp.concatenate([place_block, other_places], axis=0)
    visible = place_block[None, :] <= positions[:, None]
    outcome = attend_block(
        queries, key_block, value_block, visible, local_heads, local_tokens, score_scale
    )
    attended = (
        jnp.transpose(outcome, (1, 0, 2))
        .reshape(local_tokens, local_heads * HD)
        .astype(jnp.bfloat16)
    )
    row_width = attended.shape[1]
    row_operand = lax.all_gather(attended, "seq", axis=0, tiled=True)
    per_slice = local_tokens // head_devices
    sectioned = attended.reshape(1, per_slice, head_devices, row_width)
    sectioned = lax.all_to_all(sectioned, "head", split_axis=2, concat_axis=3, tiled=True)
    sectioned = lax.all_to_all(sectioned, "seq", split_axis=3, concat_axis=0, tiled=True)
    row_grid = row_operand.reshape(seq_devices, per_slice, head_devices, row_width)
    hessian = lax.dot_general(
        row_grid,
        lax.all_gather(sectioned, "head", axis=2, tiled=True),
        (((0, 1, 2), (0, 1, 2)), ((), ())),
        preferred_element_type=jnp.float32,
    )
    return (attended, hessian)


def solution(mesh):
    placed = (P("seq", "head"), P("seq", None), P("seq", None), P("seq"))
    return jax.shard_map(
        on_device,
        mesh=mesh,
        in_specs=placed,
        out_specs=(P("seq", "head"), P("head", "seq")),
        check_vma=False,
    )
```

profile of v0, /device:TPU:1, one launch (start us, length us, event | category | flops | bytes accessed | tf_op | source)
XLA Modules:
  0.0 303.3 jit_solution(11701521761003018919)
XLA Ops:
  7.2 0.0 copy-start
  7.2 0.0 all-gather.4.cloned.1.call-start
  7.2 4.1 %collective-permute-start = (s32[128]{0:T(128)}, s32[128]{0:T(128)S(1)}, u32[]{:S(2)}, u32[]{:S(2)}) collective-permute-start(s32[128]{0:T(128)} %param.7), channel_id=1, source_target_pairs={{0,1},{1,0},{2,3},{3,2},{4,5},{5,4},{6,7},{7,6},{8,9},{9,8},{10,11... | collective-permute-start | bytes 1544 | tf_op jit(solution)/shard_map/ppermute | solution.py:15
  11.3 0.0 copy-done
  11.4 1.9 collective-permute-start.2
  13.3 0.0 collective-permute-done
  13.3 0.7 pad_add_fusion.1
  14.0 4.9 %collective-permute-start.1 = (s32[256]{0:T(256)S(1)}, s32[256]{0:T(256)S(1)}, u32[]{:S(2)}, u32[]{:S(2)}) collective-permute-start(s32[256]{0:T(256)S(1)} %pad_add_fusion.1), channel_id=1, source_target_pairs={{0,2},{1,3},{2,0},{3,1},{4,6},{5,7},{6,4},{7,5},{8,10},{9,11},{10,... | collective-permute-start | bytes 3080 | tf_op jit(solution)/shard_map/ppermute | solution.py:15
  18.9 0.8 constant_dynamic-slice_fusion
  19.6 0.1 copy.33
  19.7 2.2 collective-permute-start.4
  22.0 1.0 copy.21
  23.0 0.1 copy.22
  23.1 0.0 collective-permute-done.1
  23.2 0.7 pad_add_fusion
  23.8 0.8 broadcast_compare_fusion
  24.6 0.0 collective-permute-done.2
  24.6 3.6 %collective-permute-start.3 = (bf16[256,128]{1,0:T(8,128)(2,1)S(1)}, bf16[256,128]{1,0:T(8,128)(2,1)S(1)}, u32[]{:S(2)}, u32[]{:S(2)}) collective-permute-start(bf16[256,128]{1,0:T(8,128)(2,1)S(1)} %pad_maximum_fusion), channel_id=1, source_target_pairs={{0,2},{1,3},{2,0},{3,1},{4,6},{5,7},{6,4},{7,5},{8,10},{9,11},{10,... | collective-permute-start | bytes 196616 | tf_op jit(solution)/shard_map/ppermute | solution.py:15
  28.3 0.0 collective-permute-done.4
  28.3 3.1 %collective-permute-start.5 = (bf16[256,128]{0,1:T(8,128)(2,1)S(1)}, bf16[256,128]{0,1:T(8,128)(2,1)S(1)}, u32[]{:S(2)}, u32[]{:S(2)}) collective-permute-start(bf16[256,128]{0,1:T(8,128)(2,1)S(1)} %pad_maximum_fusion.1), channel_id=1, source_target_pairs={{0,2},{1,3},{2,0},{3,1},{4,6},{5,7},{6,4},{7,5},{8,10},{9,11},{10,... | collective-permute-start | bytes 196616 | tf_op jit(solution)/shard_map/ppermute | solution.py:15
  31.4 0.0 collective-permute-done.3
  31.5 0.1 broadcast_in_dim.19
  31.6 0.4 fusion.23
  32.0 0.3 fusion.10
  32.3 2.5 collective-permute-done.5
  34.8 1.0 fusion.9
  35.8 0.0 all-gather.4.cloned.1.call-update
  35.8 0.0 all-gather.6.cloned.1.call-start
  35.8 1.0 copy.25
  36.9 0.1 convert_element_type.23
  36.9 0.1 copy.26
  37.1 20.3 %all_to_all.30 = bf16[1,4,32,512]{3,1,0,2:T(4,128)(2,1)S(1)} all-to-all(bf16[1,4,32,512]{3,1,0,2:T(4,128)(2,1)S(1)} %copy.26), channel_id=1, replica_groups=mesh['head'=32,'seq'=16] {'head'}, dimensions={2} | all-to-all | bytes 262144 | tf_op jit(solution)/shard_map/all_to_all | solution.py:67
  57.3 12.9 %copy.27 = bf16[1,4,1,16384]{1,2,0,3:T(2,128)(2,1)} copy(bf16[1,4,1,16384]{3,1,2,0:T(4,128)(2,1)S(1)} %bitcast.58) | data formatting | bytes 262144 | tf_op jit(solution)/shard_map/all_to_all | solution.py:67
  70.2 0.5 broadcast.33
  70.7 90.8 %reduce.2 = bf16[16384,4]{1,0:T(8,128)(2,1)} reduce(bf16[16384,1,1,4]{3,2,1,0:T(2,128)(2,1)} %bitcast.52, bf16[]{:T(256)} %broadcast.33), dimensions={1,2}, to_apply=%bitcast.45.reduce_sub_computation | reduce | bytes 262146
  161.5 8.7 %reshape.80 = bf16[16,2,2048]{2,1,0:T(2,128)(2,1)S(1)} reshape(bf16[16384,4]{1,0:T(8,128)(2,1)} %reduce.2) | data formatting | bytes 262144
  170.2 27.8 %all_to_all.31 = bf16[16,2,2048]{2,1,0:T(2,128)(2,1)S(1)} all-to-all(bf16[16,2,2048]{2,1,0:T(2,128)(2,1)S(1)} %reshape.80), channel_id=1, replica_groups=mesh['head'=32,'seq'=16] {'seq'}, dimensions={0} | all-to-all | bytes 262144 | tf_op jit(solution)/shard_map/all_to_all | solution.py:68
  198.0 12.3 %reshape.81 = bf16[16384,1,1,4]{3,2,1,0:T(2,128)(2,1)} reshape(bf16[16,2,2048]{2,1,0:T(2,128)(2,1)S(1)} %all_to_all.31) | data formatting | bytes 262144
  210.3 0.0 copy-start.1
  210.3 15.4 %copy.28 = bf16[1,4,1,16384]{3,1,2,0:T(4,128)(2,1)S(1)} copy(bf16[1,4,1,16384]{1,2,0,3:T(2,128)(2,1)} %bitcast.53) | data formatting | bytes 262144 | tf_op jit(solution)/shard_map/all_to_all | solution.py:68
  225.7 0.7 copy.42
  226.4 0.0 all-gather.6.cloned.1.call-update
  226.4 0.0 copy-done.1
  226.4 0.8 copy.31
  227.2 0.0 all-gather.4.cloned.1.call-done
  227.2 2.9 copy.24
  230.1 57.4 %all-gather.6.cloned.1.call-done = bf16[16,1,4,32,1024]{4,0,2,1,3:T(8,128)(2,1)} async-done(((bf16[16,1,4,1,1024]{4,0,2,1,3:T(8,128)(2,1)}), bf16[16,1,4,32,1024]{4,0,2,1,3:T(8,128)(2,1)}) %all-gather.6.cloned.1.call-update) | async-done | bytes 4194320 | tf_op jit(solution)/shard_map/all_gather | solution.py:72
  287.5 9.0 %fusion.3 = f32[512,1024]{1,0:T(8,128)} fusion(bf16[16,4,32,512]{3,2,1,0:T(8,128)(2,1)S(1)} %bitcast.54, bf16[16,1,4,32,1024]{4,0,2,1,3:T(8,128)(2,1)} %all-gather.6.cloned.1.call-done), kind=kOutput, calls=%fused_computation.3 | convolution fusion | flops 2147483648 | bytes 8388608 | tf_op jit(solution)/shard_map/dot_general | solution.py:70
  (3 shorter events, 0.0 us)
Async XLA Ops:
  7.2 4.2 %copy-start = (bf16[128,1024]{1,0:T(8,128)(2,1)S(1)}, bf16[128,1024]{1,0:T(8,128)(2,1)}, u32[]{:S(2)}) copy-start(bf16[128,1024]{1,0:T(8,128)(2,1)} %param.5) | copy-start | bytes 786436
  7.2 220.0 %all-gather.4.cloned.1.call-start = ((), (), s32[]{:S(2)}) async-start(), calls=%async_computation.2 | async-start | bytes 2228224 | tf_op jit(solution)/shard_map/all_gather | solution.py:64
  7.2 6.1 %collective-permute-start = (s32[128]{0:T(128)}, s32[128]{0:T(128)S(1)}, u32[]{:S(2)}, u32[]{:S(2)}) collective-permute-start(s32[128]{0:T(128)} %param.7), channel_id=1, source_target_pairs={{0,1},{1,0},{2,3},{3,2},{4,5},{5,4},{6,7},{7,6},{8,9},{9,8},{10,11... | collective-permute-start | bytes 1544 | tf_op jit(solution)/shard_map/ppermute | solution.py:15
  11.4 13.2 %collective-permute-start.2 = (bf16[128,128]{1,0:T(8,128)(2,1)S(1)}, bf16[128,128]{1,0:T(8,128)(2,1)S(1)}, u32[]{:S(2)}, u32[]{:S(2)}) collective-permute-start(bf16[128,128]{1,0:T(8,128)(2,1)S(1)} %constant_dynamic-slice_fusion.1), channel_id=1, source_target_pairs={{0,1},{1,0},{2,3},{3,2},{4,5},{5,4},{6,7},{7,6},{8,9},{9,8},{10,11... | collective-permute-start | bytes 98312 | tf_op jit(solution)/shard_map/ppermute | solution.py:15
  14.0 9.2 %collective-permute-start.1 = (s32[256]{0:T(256)S(1)}, s32[256]{0:T(256)S(1)}, u32[]{:S(2)}, u32[]{:S(2)}) collective-permute-start(s32[256]{0:T(256)S(1)} %pad_add_fusion.1), channel_id=1, source_target_pairs={{0,2},{1,3},{2,0},{3,1},{4,6},{5,7},{6,4},{7,5},{8,10},{9,11},{10,... | collective-permute-start | bytes 3080 | tf_op jit(solution)/shard_map/ppermute | solution.py:15
  19.7 8.5 %collective-permute-start.4 = (bf16[128,128]{0,1:T(8,128)(2,1)S(1)}, bf16[128,128]{0,1:T(8,128)(2,1)S(1)}, u32[]{:S(2)}, u32[]{:S(2)}) collective-permute-start(bf16[128,128]{0,1:T(8,128)(2,1)S(1)} %copy.33), channel_id=1, source_target_pairs={{0,1},{1,0},{2,3},{3,2},{4,5},{5,4},{6,7},{7,6},{8,9},{9,8},{10,11... | collective-permute-start | bytes 98312 | tf_op jit(solution)/shard_map/ppermute | solution.py:15
  24.6 6.9 %collective-permute-start.3 = (bf16[256,128]{1,0:T(8,128)(2,1)S(1)}, bf16[256,128]{1,0:T(8,128)(2,1)S(1)}, u32[]{:S(2)}, u32[]{:S(2)}) collective-permute-start(bf16[256,128]{1,0:T(8,128)(2,1)S(1)} %pad_maximum_fusion), channel_id=1, source_target_pairs={{0,2},{1,3},{2,0},{3,1},{4,6},{5,7},{6,4},{7,5},{8,10},{9,11},{10,... | collective-permute-start | bytes 196616 | tf_op jit(solution)/shard_map/ppermute | solution.py:15
  28.3 6.5 %collective-permute-start.5 = (bf16[256,128]{0,1:T(8,128)(2,1)S(1)}, bf16[256,128]{0,1:T(8,128)(2,1)S(1)}, u32[]{:S(2)}, u32[]{:S(2)}) collective-permute-start(bf16[256,128]{0,1:T(8,128)(2,1)S(1)} %pad_maximum_fusion.1), channel_id=1, source_target_pairs={{0,2},{1,3},{2,0},{3,1},{4,6},{5,7},{6,4},{7,5},{8,10},{9,11},{10,... | collective-permute-start | bytes 196616 | tf_op jit(solution)/shard_map/ppermute | solution.py:15
  35.8 251.7 %all-gather.6.cloned.1.call-start = ((), (), s32[]{:S(2)}) async-start(), calls=%async_computation.3 | async-start | bytes 4325376 | tf_op jit(solution)/shard_map/all_gather | solution.py:72
  210.3 16.1 %copy-start.1 = (bf16[128,4,128]{0,2,1:T(8,128)(2,1)S(1)}, bf16[128,4,128]{0,2,1:T(8,128)(2,1)}, u32[]{:S(2)}) copy-start(bf16[128,4,128]{0,2,1:T(8,128)(2,1)} %fusion.9) | copy-start | bytes 393220
Sparse Core Ops, SparseCore 0:
  35.9 105.3 all-gather.3
  226.5 60.8 all-gather.5
where the time goes:
time: 304 us; the launch traced here: 303 us
  other arithmetic  93.2 us (31%)
  waiting for transfers between devices  60 us (20%)
  local copies, waits for them, and re-layouts  57.5 us (19%)
  blocking collectives  48.1 us (16%)
  starting transfers between devices  20 us (7%)
  between operations  14.3 us (5%)
  matrix products  10.4 us (3%)
    unnamed x1, other arithmetic  90.8 us
    all_gather x1, waiting for transfers between devices, on_device(): lax.all_gather(sectioned, 'head', axis=2, tiled=True)  57.4 us
    all_to_all x1, blocking collectives, on_device(): lax.all_to_all(sectioned, 'seq', split_axis=3, concat_axis=0, tiled=True)  27.8 us
    unnamed x11, local copies, waits for them, and re-layouts  24.1 us
    all_to_all x1, blocking collectives, on_device(): lax.all_to_all(sectioned, 'head', split_axis=2, concat_axis=3, tiled=True)  20.3 us
    ppermute x6, starting transfers between devices, from_partner(): return lax.ppermute(value, axis, pairs)  19.9 us
    all_to_all x1, local copies, waits for them, and re-layouts, on_device(): lax.all_to_all(sectioned, 'seq', split_axis=3, concat_axis=0, tiled=True)  15.4 us
    all_to_all x1, local copies, waits for them, and re-layouts, on_device(): lax.all_to_all(sectioned, 'head', split_axis=2, concat_axis=3, tiled=True)  12.9 us
  transfers between devices with their start and end apart: 8, of which 2 were waited for; matrix products, arithmetic and copies ran while one was open for 50% of the time, Pallas kernels for 0%

commit v1 on v0

--- a/solution.py
+++ b/solution.py
@@ -65,7 +65,10 @@
     per_slice = local_tokens // head_devices
     sectioned = attended.reshape(1, per_slice, head_devices, row_width)
     sectioned = lax.all_to_all(sectioned, "head", split_axis=2, concat_axis=3, tiled=True)
-    sectioned = lax.all_to_all(sectioned, "seq", split_axis=3, concat_axis=0, tiled=True)
+    sectioned = jnp.concatenate(
+        lax.all_to_all(jnp.stack(jnp.split(sectioned, lax.axis_size("seq"), axis=3)), "seq", 0, 0),
+        axis=0,
+    )
     row_grid = row_operand.reshape(seq_devices, per_slice, head_devices, row_width)
     hessian = lax.dot_general(
         row_grid,

time: 304 us -> 237 us (0.78)
  other arithmetic: 93.2 us -> 2.42 us
  waiting for transfers between devices: 60 us -> 141 us
  local copies, waits for them, and re-layouts: 57.5 us -> 8.51 us
  blocking collectives: 48.1 us -> 29 us
  starting transfers between devices: 20 us -> 31.9 us
    unnamed x1 -> x0, other arithmetic: 90.8 us -> none
    all_gather x1, waiting for transfers between devices: 0.01 us -> 65.2 us  [on_device(): row_operand = lax.all_gather(attended, 'seq', axis=0, tiled=True)]
    all_to_all x2 -> x1, local copies, waits for them, and re-layouts: 28.3 us -> 0.69 us  [on_device(): lax.all_to_all(jnp.stack(jnp.split(sectioned, lax.axis_size('seq'), axis=...]
    unnamed x11 -> x22, local copies, waits for them, and re-layouts: 24.1 us -> 3 us
    all_to_all x2 -> x1, blocking collectives: 48.1 us -> 29 us  [on_device(): lax.all_to_all(jnp.stack(jnp.split(sectioned, lax.axis_size('seq'), axis=...]
    all_to_all x0 -> x1, starting transfers between devices: none -> 11.9 us  [on_device(): lax.all_to_all(sectioned, 'head', split_axis=2, concat_axis=3, tiled=True)]
    all_to_all x0 -> x1, waiting for transfers between devices: none -> 7.76 us  [on_device(): lax.all_to_all(sectioned, 'head', split_axis=2, concat_axis=3, tiled=True)]
    all_gather x1, waiting for transfers between devices: 57.4 us -> 64.4 us  [on_device(): lax.all_gather(sectioned, 'head', axis=2, tiled=True)]
  transfers between devices with their start and end apart: 8 -> 9, of which waited for: 2 -> 4; matrix products, arithmetic and copies ran while one was open for 50% -> 4% of each run, Pallas kernels for 0% -> 0%
where the time goes in v1:
time: 237 us
  waiting for transfers between devices  141 us (59%)
  starting transfers between devices  31.9 us (13%)
  blocking collectives  29 us (12%)
  between operations  14.3 us (6%)
  matrix products  9.76 us (4%)
  local copies, waits for them, and re-layouts  8.51 us (4%)
  other arithmetic  2.42 us (1%)
    all_gather x1, waiting for transfers between devices, on_device(): row_operand = lax.all_gather(attended, 'seq', axis=0, tiled=True)  65.2 us
    all_gather x1, waiting for transfers between devices, on_device(): lax.all_gather(sectioned, 'head', axis=2, tiled=True)  64.4 us
    all_to_all x1, blocking collectives, on_device(): lax.all_to_all(jnp.stack(jnp.split(sectioned, lax.axis_size('seq'), axis=...  29 us
    ppermute x6, starting transfers between devices, from_partner(): return lax.ppermute(value, axis, pairs)  19.9 us
    all_to_all x1, starting transfers between devices, on_device(): lax.all_to_all(sectioned, 'head', split_axis=2, concat_axis=3, tiled=True)  11.9 us
    dot_general x1, matrix products, on_device(): lax.dot_general(row_grid, lax.all_gather(sectioned, 'head', axis=2, tiled...  9.04 us
    all_to_all x1, waiting for transfers between devices, on_device(): lax.all_to_all(sectioned, 'head', split_axis=2, concat_axis=3, tiled=True)  7.76 us
  transfers between devices with their start and end apart: 9, of which 4 were waited for; matrix products, arithmetic and copies ran while one was open for 4% of the time, Pallas kernels for 0%

profile of v1, /device:TPU:1, one launch (start us, length us, event | category | flops | bytes accessed | tf_op | source)
XLA Modules:
  0.0 236.5 jit_solution(2556307770038450139)
XLA Ops:
  7.2 0.0 copy-start
  7.2 4.1 %collective-permute-start = (s32[128]{0:T(128)}, s32[128]{0:T(128)S(1)}, u32[]{:S(2)}, u32[]{:S(2)}) collective-permute-start(s32[128]{0:T(128)} %param.7), channel_id=1, source_target_pairs={{0,1},{1,0},{2,3},{3,2},{4,5},{5,4},{6,7},{7,6},{8,9},{9,8},{10,11... | collective-permute-start | bytes 1544 | tf_op jit(solution)/shard_map/ppermute | solution.py:15
  11.3 0.0 copy-done
  11.3 0.1 copy.370
  11.4 1.9 collective-permute-start.4
  13.4 0.0 collective-permute-done
  13.4 0.7 pad_add_fusion.1
  14.0 4.9 %collective-permute-start.1 = (s32[256]{0:T(256)S(1)}, s32[256]{0:T(256)S(1)}, u32[]{:S(2)}, u32[]{:S(2)}) collective-permute-start(s32[256]{0:T(256)S(1)} %pad_add_fusion.1), channel_id=1, source_target_pairs={{0,2},{1,3},{2,0},{3,1},{4,6},{5,7},{6,4},{7,5},{8,10},{9,11},{10,... | collective-permute-start | bytes 3080 | tf_op jit(solution)/shard_map/ppermute | solution.py:15
  18.9 0.8 constant_dynamic-slice_fusion.1
  19.7 2.2 collective-permute-start.2
  21.9 1.0 copy.360
  22.9 0.1 copy.361
  23.1 0.0 collective-permute-done.1
  23.1 0.7 pad_add_fusion
  23.8 0.8 broadcast_compare_fusion
  24.5 0.0 collective-permute-done.2
  24.6 3.6 %collective-permute-start.3 = (bf16[256,128]{1,0:T(8,128)(2,1)S(1)}, bf16[256,128]{1,0:T(8,128)(2,1)S(1)}, u32[]{:S(2)}, u32[]{:S(2)}) collective-permute-start(bf16[256,128]{1,0:T(8,128)(2,1)S(1)} %pad_maximum_fusion), channel_id=1, source_target_pairs={{0,2},{1,3},{2,0},{3,1},{4,6},{5,7},{6,4},{7,5},{8,10},{9,11},{10,... | collective-permute-start | bytes 196616 | tf_op jit(solution)/shard_map/ppermute | solution.py:15
  28.2 0.0 collective-permute-done.4
  28.2 3.1 %collective-permute-start.5 = (bf16[256,128]{0,1:T(8,128)(2,1)S(1)}, bf16[256,128]{0,1:T(8,128)(2,1)S(1)}, u32[]{:S(2)}, u32[]{:S(2)}) collective-permute-start(bf16[256,128]{0,1:T(8,128)(2,1)S(1)} %pad_maximum_fusion.1), channel_id=1, source_target_pairs={{0,2},{1,3},{2,0},{3,1},{4,6},{5,7},{6,4},{7,5},{8,10},{9,11},{10,... | collective-permute-start | bytes 196616 | tf_op jit(solution)/shard_map/ppermute | solution.py:15
  31.4 0.0 collective-permute-done.3
  31.4 0.1 broadcast_in_dim.19
  31.5 0.4 fusion.23
  31.9 0.3 fusion.10
  32.2 2.5 %collective-permute-done.5 = bf16[256,128]{0,1:T(8,128)(2,1)S(1)} collective-permute-done((bf16[256,128]{0,1:T(8,128)(2,1)S(1)}, bf16[256,128]{0,1:T(8,128)(2,1)S(1)}, u32[]{:S(2)}, u32[]{:S(2)}) %collective-permute-start.5) | collective-permute-done | bytes 65568 | tf_op jit(solution)/shard_map/ppermute | solution.py:15
  34.7 0.3 fusion.9
  35.1 0.0 copy-start.1
  35.1 0.1 copy.364
  35.2 0.1 convert_element_type.23
  35.3 0.8 copy.365
  36.1 11.9 %all-to-all-start = ((bf16[1,4,32,512]{3,1,0,2:T(4,128)(2,1)}), bf16[1,4,32,512]{3,1,0,2:T(4,128)(2,1)S(1)}, u32[]{:S(2)}, u32[]{:S(2)}) async-start(bf16[1,4,32,512]{3,1,0,2:T(4,128)(2,1)} %copy.365), calls=%async_computation | async-start | bytes 262144 | tf_op jit(solution)/shard_map/all_to_all | solution.py:67
  48.0 0.0 all-gather.4.cloned.1.call-start
  48.0 0.0 copy-done.1
  48.0 0.7 all-gather.4.cloned.1.call-update
  48.7 0.0 all-gather.6.cloned.1.call-start
  48.8 7.8 %all-to-all-done = bf16[1,4,32,512]{3,1,0,2:T(4,128)(2,1)S(1)} async-done(((bf16[1,4,32,512]{3,1,0,2:T(4,128)(2,1)}), bf16[1,4,32,512]{3,1,0,2:T(4,128)(2,1)S(1)}, u32[]{:S(2)}, u32[]{:S(2)}) %all-to-all-start) | async-done | bytes 131104 | tf_op jit(solution)/shard_map/all_to_all | solution.py:67
  56.8 29.0 %all_to_all.17 = bf16[16,1,4,1,1024]{4,2,3,1,0:T(4,128)(2,1)S(1)} all-to-all(bf16[16,1,4,1,1024]{4,2,3,1,0:T(4,128)(2,1)S(1)} %constant_dynamic-update-slice_fusion), channel_id=1, replica_groups=mesh['head'=32,'seq'=16] {'seq'}, dimensions={0} | all-to-all | bytes 262144 | tf_op jit(solution)/shard_map/all_to_all | solution.py:69
  85.8 0.7 copy.366
  86.5 0.0 all-gather.6.cloned.1.call-update
  86.5 1.7 copy.368
  88.2 65.2 %all-gather.4.cloned.1.call-done = bf16[2048,512]{0,1:T(8,128)(2,1)} async-done(((bf16[128,512]{0,1:T(8,128)(2,1)}), bf16[2048,512]{0,1:T(8,128)(2,1)}) %all-gather.4.cloned.1.call-update) | async-done | bytes 2097168 | tf_op jit(solution)/shard_map/all_gather | solution.py:64
  153.4 2.9 %copy.363 = bf16[2048,512]{1,0:T(8,128)(2,1)S(1)} copy(bf16[2048,512]{0,1:T(8,128)(2,1)} %all-gather.4.cloned.1.call-done) | data formatting | bytes 4194304 | tf_op jit(solution)/shard_map/all_gather | solution.py:64
  156.2 64.4 %all-gather.6.cloned.1.call-done = bf16[16,1,4,32,1024]{4,0,2,1,3:T(8,128)(2,1)} async-done(((bf16[16,1,4,1,1024]{4,0,2,1,3:T(8,128)(2,1)}), bf16[16,1,4,32,1024]{4,0,2,1,3:T(8,128)(2,1)}) %all-gather.6.cloned.1.call-update) | async-done | bytes 4194320 | tf_op jit(solution)/shard_map/all_gather | solution.py:75
  220.6 9.0 %fusion.3 = f32[512,1024]{1,0:T(8,128)} fusion(bf16[16,4,32,512]{3,2,1,0:T(8,128)(2,1)S(1)} %bitcast.101, bf16[16,1,4,32,1024]{4,0,2,1,3:T(8,128)(2,1)} %all-gather.6.cloned.1.call-done), kind=kOutput, calls=%fused_computation.3 | convolution fusion | flops 2147483648 | bytes 8388608 | tf_op jit(solution)/shard_map/dot_general | solution.py:73
  (19 shorter events, 0.2 us)
Async XLA Ops:
  7.2 4.1 %copy-start = (bf16[128,1024]{1,0:T(8,128)(2,1)S(1)}, bf16[128,1024]{1,0:T(8,128)(2,1)}, u32[]{:S(2)}) copy-start(bf16[128,1024]{1,0:T(8,128)(2,1)} %param.6) | copy-start | bytes 786436
  7.2 6.2 %collective-permute-start = (s32[128]{0:T(128)}, s32[128]{0:T(128)S(1)}, u32[]{:S(2)}, u32[]{:S(2)}) collective-permute-start(s32[128]{0:T(128)} %param.7), channel_id=1, source_target_pairs={{0,1},{1,0},{2,3},{3,2},{4,5},{5,4},{6,7},{7,6},{8,9},{9,8},{10,11... | collective-permute-start | bytes 1544 | tf_op jit(solution)/shard_map/ppermute | solution.py:15
  11.4 16.8 %collective-permute-start.4 = (bf16[128,128]{0,1:T(8,128)(2,1)S(1)}, bf16[128,128]{0,1:T(8,128)(2,1)S(1)}, u32[]{:S(2)}, u32[]{:S(2)}) collective-permute-start(bf16[128,128]{0,1:T(8,128)(2,1)S(1)} %copy.370), channel_id=1, source_target_pairs={{0,1},{1,0},{2,3},{3,2},{4,5},{5,4},{6,7},{7,6},{8,9},{9,8},{10,11... | collective-permute-start | bytes 98312 | tf_op jit(solution)/shard_map/ppermute | solution.py:15
  14.0 9.1 %collective-permute-start.1 = (s32[256]{0:T(256)S(1)}, s32[256]{0:T(256)S(1)}, u32[]{:S(2)}, u32[]{:S(2)}) collective-permute-start(s32[256]{0:T(256)S(1)} %pad_add_fusion.1), channel_id=1, source_target_pairs={{0,2},{1,3},{2,0},{3,1},{4,6},{5,7},{6,4},{7,5},{8,10},{9,11},{10,... | collective-permute-start | bytes 3080 | tf_op jit(solution)/shard_map/ppermute | solution.py:15
  19.7 4.8 %collective-permute-start.2 = (bf16[128,128]{1,0:T(8,128)(2,1)S(1)}, bf16[128,128]{1,0:T(8,128)(2,1)S(1)}, u32[]{:S(2)}, u32[]{:S(2)}) collective-permute-start(bf16[128,128]{1,0:T(8,128)(2,1)S(1)} %constant_dynamic-slice_fusion.1), channel_id=1, source_target_pairs={{0,1},{1,0},{2,3},{3,2},{4,5},{5,4},{6,7},{7,6},{8,9},{9,8},{10,11... | collective-permute-start | bytes 98312 | tf_op jit(solution)/shard_map/ppermute | solution.py:15
  24.6 6.9 %collective-permute-start.3 = (bf16[256,128]{1,0:T(8,128)(2,1)S(1)}, bf16[256,128]{1,0:T(8,128)(2,1)S(1)}, u32[]{:S(2)}, u32[]{:S(2)}) collective-permute-start(bf16[256,128]{1,0:T(8,128)(2,1)S(1)} %pad_maximum_fusion), channel_id=1, source_target_pairs={{0,2},{1,3},{2,0},{3,1},{4,6},{5,7},{6,4},{7,5},{8,10},{9,11},{10,... | collective-permute-start | bytes 196616 | tf_op jit(solution)/shard_map/ppermute | solution.py:15
  28.2 6.5 %collective-permute-start.5 = (bf16[256,128]{0,1:T(8,128)(2,1)S(1)}, bf16[256,128]{0,1:T(8,128)(2,1)S(1)}, u32[]{:S(2)}, u32[]{:S(2)}) collective-permute-start(bf16[256,128]{0,1:T(8,128)(2,1)S(1)} %pad_maximum_fusion.1), channel_id=1, source_target_pairs={{0,2},{1,3},{2,0},{3,1},{4,6},{5,7},{6,4},{7,5},{8,10},{9,11},{10,... | collective-permute-start | bytes 196616 | tf_op jit(solution)/shard_map/ppermute | solution.py:15
  35.1 13.0 %copy-start.1 = (bf16[128,4,128]{0,2,1:T(8,128)(2,1)}, bf16[128,4,128]{0,2,1:T(8,128)(2,1)S(1)}, u32[]{:S(2)}) copy-start(bf16[128,4,128]{0,2,1:T(8,128)(2,1)S(1)} %fusion.9) | copy-start | bytes 393220
  36.1 20.5 %all-to-all-start = ((bf16[1,4,32,512]{3,1,0,2:T(4,128)(2,1)}), bf16[1,4,32,512]{3,1,0,2:T(4,128)(2,1)S(1)}, u32[]{:S(2)}, u32[]{:S(2)}) async-start(bf16[1,4,32,512]{3,1,0,2:T(4,128)(2,1)} %copy.365), calls=%async_computation | async-start | bytes 262144 | tf_op jit(solution)/shard_map/all_to_all | solution.py:67
  48.0 105.4 %all-gather.4.cloned.1.call-start = ((), (), s32[]{:S(2)}) async-start(), calls=%async_computation.2 | async-start | bytes 2228224 | tf_op jit(solution)/shard_map/all_gather | solution.py:64
  48.7 171.9 %all-gather.6.cloned.1.call-start = ((), (), s32[]{:S(2)}) async-start(), calls=%async_computation.3 | async-start | bytes 4325376 | tf_op jit(solution)/shard_map/all_gather | solution.py:75
Sparse Core Ops, SparseCore 0:
  52.4 100.9 all-gather.3
  155.5 65.0 all-gather.5
